TPU v7x, 32 devices: a whole 2x2x4 slice. The times are simulated.
32 devices in a mesh: dp: 8 (over z, x), feat: 4 (over y, core).
Axes of the slice: x: 2, y: 2, z: 4, core: 2. Of those that a mesh axis runs over, the one named last changes fastest.
Arguments:
- samples: bfloat16 [8192, 1024], P('dp', 'feat'), may hold values from -6 to 6
- freqs: bfloat16 [1024, 32768], P('dp', 'feat'), may hold values from -0.1875 to 0.1875
- phases: float32 [32768], P('feat'), may hold values from -3.140625 to 3.140625
- range_test: bfloat16 [32768, 256], P('feat'), may hold values from -6 to 6
- corange_test: bfloat16 [256, 8192], P(None, 'dp'), may hold values from -6 to 6
Outputs:
- range_sketch: float32 [8192, 256], P(('dp', 'feat'))
- corange_sketch: float32 [256, 32768], P('dp', 'feat')
All inputs are finite; a program needn't handle non-finite values.
Results may differ from a plain program's by a relative error of at most 0.0024.
Values may be sent and summed in bfloat16 or wider, within the bound.
A program may use at most 128 MiB of HBM per device.

v0:
```python
import math
import jax
import jax.numpy as jnp
from jax import lax
from jax.sharding import PartitionSpec as P


def on_device(samples, freqs, phases, range_test, corange_test):
    gathered = lax.all_gather(samples, "feat", axis=1, tiled=True)
    feature_count = freqs.shape[1]
    projection = jnp.dot(
        gathered,
        lax.all_gather(freqs, "dp", axis=0, tiled=True),
        preferred_element_type=jnp.float32,
    )
    scale = math.sqrt(2.0 / (feature_count * lax.axis_size("feat")))
    features = (scale * jnp.cos(projection + phases[None, :])).astype(jnp.bfloat16)
    range_sketch = lax.psum_scatter(
        jnp.dot(features, range_test, preferred_element_type=jnp.float32),
        "feat",
        scatter_dimension=0,
        tiled=True,
    )
    corange_sketch = lax.psum_scatter(
        jnp.dot(corange_test, features, preferred_element_type=jnp.float32),
        "dp",
        scatter_dimension=0,
        tiled=True,
    )
    return (range_sketch, corange_sketch)


def solution(mesh):
    placed = (P("dp", "feat"), P("dp", "feat"), P("feat"), P("feat", None), P(None, "dp"))
    return jax.shard_map(
        on_device,
        mesh=mesh,
        in_specs=placed,
        out_specs=(P(("dp", "feat"), None), P("dp", "feat")),
        check_vma=False,
    )
```

profile of v0, /device:TPU:0, one launch (start us, length us, event | category | flops | bytes accessed | tf_op | source)
XLA Modules:
  0.0 583.5 jit_solution(11586309907684146967)
XLA Ops:
  7.2 0.0 copy-start
  7.2 0.0 all-gather.3.cloned.1.call-start
  7.2 0.7 all-gather.3.cloned.1.call-update
  7.9 0.0 all-gather.5.cloned.1.call-start
  8.0 0.7 all-gather.5.cloned.1.call-update
  8.7 0.0 reduce-scatter.5.cloned.1.call-start
  8.7 26.4 %all-gather.3.cloned.1.call-done = bf16[1024,1024]{1,0:T(8,128)(2,1)} async-done(((bf16[1024,256]{1,0:T(8,128)(2,1)}), bf16[1024,1024]{1,0:T(8,128)(2,1)}) %all-gather.3.cloned.1.call-update) | async-done | bytes 2097168 | tf_op jit(solution)/shard_map/all_gather | solution.py:9
  35.1 229.8 %all-gather.5.cloned.1.call-done = bf16[1024,8192]{1,0:T(8,128)(2,1)} async-done(((bf16[128,8192]{1,0:T(8,128)(2,1)}), bf16[1024,8192]{1,0:T(8,128)(2,1)}) %all-gather.5.cloned.1.call-update) | async-done | bytes 16777232 | tf_op jit(solution)/shard_map/all_gather | solution.py:13
  264.9 0.0 copy-start.1
  264.9 124.0 %multiply_convert_fusion = bf16[1024,8192]{1,0:T(8,128)(2,1)S(1)} fusion(bf16[1024,1024]{1,0:T(8,128)(2,1)} %all-gather.3.cloned.1.call-done, bf16[1024,8192]{1,0:T(8,128)(2,1)} %all-gather.5.cloned.1.call-done, f32[8192]{0:T(1024)} %param.7), kind=kOutput, calls=%fused_computation | convolution fusion | flops 17205035008 | bytes 35684352 | tf_op jit(solution)/shard_map/dot_general | solution.py:11
  388.9 0.0 copy-start.2
  388.9 5.7 copy-done.2
  394.6 0.0 copy-done.1
  394.6 5.5 fusion
  400.2 0.0 reduce-scatter.5.cloned.1.call-update
  400.2 0.0 reduce-scatter.7.cloned.1.call-start
  400.2 0.0 copy-done
  400.3 14.1 %convolution_bitcast_fusion = f32[256,8192]{0,1:T(8,128)} fusion(bf16[1024,8192]{1,0:T(8,128)(2,1)} %copy-done.2, bf16[256,1024]{1,0:T(8,128)(2,1)S(1)} %copy-done), kind=kOutput, calls=%fused_computation.1 | convolution fusion | flops 4294967296 | bytes 25690112 | tf_op jit(solution)/shard_map/dot_general | solution.py:25
  414.3 9.0 %copy.9 = f32[256,8192]{1,0:T(8,128)} copy(f32[256,8192]{0,1:T(8,128)} %convolution_bitcast_fusion) | data formatting | bytes 16777216
  423.3 0.0 reduce-scatter.7.cloned.1.call-update
  423.3 0.1 reduce-scatter.5.cloned.1.call-done
  423.4 153.5 %reduce-scatter.7.cloned.1.call-done = f32[32,8192]{1,0:T(8,128)} async-done(((f32[256,8192]{1,0:T(8,128)}), f32[32,8192]{1,0:T(8,128)}) %reduce-scatter.7.cloned.1.call-update) | async-done | bytes 1048592
Async XLA Ops:
  7.2 393.1 %copy-start = (bf16[256,1024]{1,0:T(8,128)(2,1)S(1)}, bf16[256,1024]{1,0:T(8,128)(2,1)}, u32[]{:S(2)}) copy-start(bf16[256,1024]{1,0:T(8,128)(2,1)} %param.9) | copy-start | bytes 1572868
  7.2 28.0 %all-gather.3.cloned.1.call-start = ((), (), s32[]{:S(2)}) async-start(), calls=%async_computation.2 | async-start | bytes 2621440 | tf_op jit(solution)/shard_map/all_gather | solution.py:9
  7.9 257.0 %all-gather.5.cloned.1.call-start = ((), (), s32[]{:S(2)}) async-start(), calls=%async_computation.3 | async-start | bytes 18874368 | tf_op jit(solution)/shard_map/all_gather | solution.py:13
  8.7 414.8 %reduce-scatter.5.cloned.1.call-start = ((), (), s32[]{:S(2)}) async-start(), calls=%async_computation.4 | async-start | bytes 1310720 | tf_op jit(solution)/shard_map/reduce_scatter | solution.py:18
  264.9 129.7 %copy-start.1 = (bf16[8192,256]{1,0:T(8,128)(2,1)S(1)}, bf16[8192,256]{1,0:T(8,128)(2,1)}, u32[]{:S(2)}) copy-start(bf16[8192,256]{1,0:T(8,128)(2,1)} %param.8) | copy-start | bytes 12582916
  388.9 5.7 copy-start.2
  400.2 176.8 %reduce-scatter.7.cloned.1.call-start = ((), (), s32[]{:S(2)}) async-start(), calls=%async_computation.5 | async-start | bytes 9437184
Sparse Core Ops, SparseCore 0:
  9.6 25.5 all-gather.2
  37.3 227.5 all-gather.4
  400.3 23.0 reduce-scatter.4
  427.9 149.0 reduce-scatter.6
where the time goes:
time: 584 us
  waiting for transfers between devices  411 us (70%)
  matrix products  144 us (25%)
  local copies, waits for them, and re-layouts  14.7 us (3%)
  between operations  13.8 us (2%)
    all_gather x1, waiting for transfers between devices, on_device(): lax.all_gather(freqs, 'dp', axis=0, tiled=True)  230 us
    unnamed x5, waiting for transfers between devices  155 us
    dot_general x1, matrix products, on_device(): jnp.dot(gathered, lax.all_gather(freqs, 'dp', axis=0, tiled=True), prefer...  124 us
    all_gather x1, waiting for transfers between devices, on_device(): gathered = lax.all_gather(samples, 'feat', axis=1, tiled=True)  26.4 us
    unnamed x7, local copies, waits for them, and re-layouts  14.7 us
    dot_general x1, matrix products, on_device(): jnp.dot(corange_test, features, preferred_element_type=jnp.float32)  14.1 us
  transfers between devices with their start and end apart: 4, of which 4 were waited for; matrix products, arithmetic and copies ran while one was open for 4% of the time, Pallas kernels for 0%

commit v1 on v0

--- a/solution.py
+++ b/solution.py
@@ -5,8 +5,19 @@
 from jax.sharding import PartitionSpec as P
 
 
+def pass_along(x, mesh_axis, d):
+    size = lax.axis_size(mesh_axis)
+    right = [(i, (i + 1) % size) for i in range(size)]
+    shards = [x]
+    for far in range(1, size):
+        shards = [lax.ppermute(shards[0], mesh_axis, right), *shards]
+    whole = jnp.concatenate(shards, axis=d)
+    shift = (lax.axis_index(mesh_axis) + 1) * shards[-1].shape[d]
+    return jnp.roll(whole, shift, axis=d)
+
+
 def on_device(samples, freqs, phases, range_test, corange_test):
-    gathered = lax.all_gather(samples, "feat", axis=1, tiled=True)
+    gathered = pass_along(samples, "feat", 1)
     feature_count = freqs.shape[1]
     projection = jnp.dot(
         gathered,

time: 584 us -> 559 us (0.957)
  waiting for transfers between devices: 411 us -> 379 us
  local copies, waits for them, and re-layouts: 14.7 us -> 21.7 us
    all_gather x1, waiting for transfers between devices: 230 us -> 199 us  [on_device(): lax.all_gather(freqs, 'dp', axis=0, tiled=True)]
    all_gather x1 -> x0, waiting for transfers between devices: 26.4 us -> none  [on_device(): gathered = lax.all_gather(samples, 'feat', axis=1, tiled=True)]
    ppermute x0 -> x3, waiting for transfers between devices: none -> 26.2 us  [pass_along(): shards = [lax.ppermute(shards[0], mesh_axis, right), *shards]]
    unnamed x7 -> x18, local copies, waits for them, and re-layouts: 14.7 us -> 20.8 us
    unnamed x5 -> x4, waiting for transfers between devices: 155 us -> 154 us
  transfers between devices with their start and end apart: 4 -> 6, of which waited for: 4 -> 6; matrix products, arithmetic and copies ran while one was open for 4% -> 5% of each run, Pallas kernels for 0% -> 0%
where the time goes in v1:
time: 559 us
  waiting for transfers between devices  379 us (68%)
  matrix products  144 us (26%)
  local copies, waits for them, and re-layouts  21.7 us (4%)
  between operations  13.8 us (2%)
    all_gather x1, waiting for transfers between devices, on_device(): lax.all_gather(freqs, 'dp', axis=0, tiled=True)  199 us
    unnamed x4, waiting for transfers between devices  154 us
    dot_general x1, matrix products, on_device(): jnp.dot(gathered, lax.all_gather(freqs, 'dp', axis=0, tiled=True), prefer...  124 us
    ppermute x3, waiting for transfers between devices, pass_along(): shards = [lax.ppermute(shards[0], mesh_axis, right), *shards]  26.2 us
    unnamed x18, local copies, waits for them, and re-layouts  20.8 us
    dot_general x1, matrix products, on_device(): jnp.dot(corange_test, features, preferred_element_type=jnp.float32)  14.1 us
  transfers between devices with their start and end apart: 6, of which 6 were waited for; matrix products, arithmetic and copies ran while one was open for 5% of the time, Pallas kernels for 0%

profile of v1, /device:TPU:0, one launch (start us, length us, event | category | flops | bytes accessed | tf_op | source)
XLA Modules:
  0.0 559.2 jit_solution(17624162532017299338)
XLA Ops:
  7.2 0.0 copy-start
  7.2 0.0 copy-start.1
  7.2 0.0 all-gather.2.cloned.1.call-start
  7.2 0.7 all-gather.2.cloned.1.call-update
  7.9 0.0 reduce-scatter.5.cloned.1.call-start
  8.0 0.5 collective-permute-start
  8.5 9.0 %collective-permute-done = bf16[1024,256]{1,0:T(8,128)(2,1)S(1)} collective-permute-done((bf16[1024,256]{1,0:T(8,128)(2,1)}, bf16[1024,256]{1,0:T(8,128)(2,1)S(1)}, u32[]{:S(2)}, u32[]{:S(2)}) %collective-permute-start) | collective-permute-done | bytes 524320 | tf_op jit(solution)/shard_map/ppermute | solution.py:13
  17.5 0.0 collective-permute-start.1
  17.5 8.6 %collective-permute-done.1 = bf16[1024,256]{1,0:T(8,128)(2,1)S(1)} collective-permute-done((bf16[1024,256]{1,0:T(8,128)(2,1)S(1)}, bf16[1024,256]{1,0:T(8,128)(2,1)S(1)}, u32[]{:S(2)}, u32[]{:S(2)}) %collective-permute-start.1) | collective-permute-done | bytes 524320 | tf_op jit(solution)/shard_map/ppermute | solution.py:13
  26.1 0.0 collective-permute-start.2
  26.1 0.0 copy-start.3
  26.1 8.6 %collective-permute-done.2 = bf16[1024,256]{1,0:T(8,128)(2,1)S(1)} collective-permute-done((bf16[1024,256]{1,0:T(8,128)(2,1)S(1)}, bf16[1024,256]{1,0:T(8,128)(2,1)S(1)}, u32[]{:S(2)}, u32[]{:S(2)}) %collective-permute-start.2) | collective-permute-done | bytes 524320 | tf_op jit(solution)/shard_map/ppermute | solution.py:13
  34.7 0.9 constant_dynamic-update-slice_fusion.7
  35.6 0.9 constant_dynamic-update-slice_fusion.6
  36.4 0.9 constant_dynamic-update-slice_fusion.5
  37.3 0.0 copy-done.1
  37.3 0.9 constant_dynamic-update-slice_fusion.4
  38.2 0.9 constant_dynamic-update-slice_fusion.3
  39.1 0.9 constant_dynamic-update-slice_fusion.2
  40.0 0.9 constant_dynamic-update-slice_fusion.1
  40.8 0.9 constant_dynamic-update-slice_fusion
  41.7 198.8 %all-gather.2.cloned.1.call-done = bf16[1024,8192]{1,0:T(8,128)(2,1)} async-done(((bf16[128,8192]{1,0:T(8,128)(2,1)}), bf16[1024,8192]{1,0:T(8,128)(2,1)}) %all-gather.2.cloned.1.call-update) | async-done | bytes 16777232 | tf_op jit(solution)/shard_map/all_gather | solution.py:24
  240.5 0.0 copy-done.3
  240.5 0.0 copy-start.2
  240.5 123.9 %multiply_convert_fusion = bf16[1024,8192]{1,0:T(8,128)(2,1)S(1)} fusion(bf16[1024,8192]{1,0:T(8,128)(2,1)} %all-gather.2.cloned.1.call-done, f32[8192]{0:T(1024)S(1)} %copy-done.3, bf16[1024,2048]{1,0:T(8,128)(2,1)} %constant_dynamic-update-slice_fusion, s32[]{:T(128)S(6)} %select_n.14), kind=kOutput, calls=%fused_computation | convolution fusion | flops 17205035008 | bytes 35684356 | tf_op jit(solution)/shard_map/dot_general | solution.py:22
  364.4 0.0 copy-start.4
  364.4 5.7 %copy-done.4 = bf16[1024,8192]{1,0:T(8,128)(2,1)} copy-done((bf16[1024,8192]{1,0:T(8,128)(2,1)}, bf16[1024,8192]{1,0:T(8,128)(2,1)S(1)}, u32[]{:S(2)}) %copy-start.4) | copy-done | bytes 16777240
  370.1 0.0 copy-done.2
  370.1 5.6 fusion.2
  375.7 0.0 reduce-scatter.5.cloned.1.call-update
  375.7 0.0 reduce-scatter.7.cloned.1.call-start
  375.8 0.0 copy-done
  375.8 14.1 %convolution_bitcast_fusion = f32[256,8192]{0,1:T(8,128)} fusion(bf16[1024,8192]{1,0:T(8,128)(2,1)} %copy-done.4, bf16[256,1024]{1,0:T(8,128)(2,1)S(1)} %copy-done), kind=kOutput, calls=%fused_computation.1 | convolution fusion | flops 4294967296 | bytes 25690112 | tf_op jit(solution)/shard_map/dot_general | solution.py:36
  389.9 9.0 %copy.9 = f32[256,8192]{1,0:T(8,128)} copy(f32[256,8192]{0,1:T(8,128)} %convolution_bitcast_fusion) | data formatting | bytes 16777216
  398.8 0.0 reduce-scatter.7.cloned.1.call-update
  398.8 0.1 reduce-scatter.5.cloned.1.call-done
  398.9 153.7 %reduce-scatter.7.cloned.1.call-done = f32[32,8192]{1,0:T(8,128)} async-done(((f32[256,8192]{1,0:T(8,128)}), f32[32,8192]{1,0:T(8,128)}) %reduce-scatter.7.cloned.1.call-update) | async-done | bytes 1048592
Async XLA Ops:
  7.2 368.6 %copy-start = (bf16[256,1024]{1,0:T(8,128)(2,1)S(1)}, bf16[256,1024]{1,0:T(8,128)(2,1)}, u32[]{:S(2)}) copy-start(bf16[256,1024]{1,0:T(8,128)(2,1)} %param.9) | copy-start | bytes 1572868
  7.2 30.1 %copy-start.1 = (bf16[1024,256]{1,0:T(8,128)(2,1)S(1)}, bf16[1024,256]{1,0:T(8,128)(2,1)}, u32[]{:S(2)}) copy-start(bf16[1024,256]{1,0:T(8,128)(2,1)} %param.5) | copy-start | bytes 1572868
  7.2 233.3 %all-gather.2.cloned.1.call-start = ((), (), s32[]{:S(2)}) async-start(), calls=%async_computation.2 | async-start | bytes 18874368 | tf_op jit(solution)/shard_map/all_gather | solution.py:24
  7.9 391.0 %reduce-scatter.5.cloned.1.call-start = ((), (), s32[]{:S(2)}) async-start(), calls=%async_computation.3 | async-start | bytes 1310720 | tf_op jit(solution)/shard_map/reduce_scatter | solution.py:29
  8.0 9.5 %collective-permute-start = (bf16[1024,256]{1,0:T(8,128)(2,1)}, bf16[1024,256]{1,0:T(8,128)(2,1)S(1)}, u32[]{:S(2)}, u32[]{:S(2)}) collective-permute-start(bf16[1024,256]{1,0:T(8,128)(2,1)} %param.5), channel_id=1, source_target_pairs={{0,1},{1,2},{2,3},{3,0},{4,5},{5,6},{6,7},{7,4},{8,9},{9,10},{10,1... | collective-permute-start | bytes 1572872 | tf_op jit(solution)/shard_map/ppermute | solution.py:13
  17.5 8.6 %collective-permute-start.1 = (bf16[1024,256]{1,0:T(8,128)(2,1)S(1)}, bf16[1024,256]{1,0:T(8,128)(2,1)S(1)}, u32[]{:S(2)}, u32[]{:S(2)}) collective-permute-start(bf16[1024,256]{1,0:T(8,128)(2,1)S(1)} %collective-permute-done), channel_id=1, source_target_pairs={{0,1},{1,2},{2,3},{3,0},{4,5},{5,6},{6,7},{7,4},{8,9},{9,10},{10,1... | collective-permute-start | bytes 1572872 | tf_op jit(solution)/shard_map/ppermute | solution.py:13
  26.1 8.6 %collective-permute-start.2 = (bf16[1024,256]{1,0:T(8,128)(2,1)S(1)}, bf16[1024,256]{1,0:T(8,128)(2,1)S(1)}, u32[]{:S(2)}, u32[]{:S(2)}) collective-permute-start(bf16[1024,256]{1,0:T(8,128)(2,1)S(1)} %collective-permute-done.1), channel_id=1, source_target_pairs={{0,1},{1,2},{2,3},{3,0},{4,5},{5,6},{6,7},{7,4},{8,9},{9,10},{10,1... | collective-permute-start | bytes 1572872 | tf_op jit(solution)/shard_map/ppermute | solution.py:13
  26.1 214.4 %copy-start.3 = (f32[8192]{0:T(1024)S(1)}, f32[8192]{0:T(1024)}, u32[]{:S(2)}) copy-start(f32[8192]{0:T(1024)} %param.7) | copy-start | bytes 98308
  240.5 129.7 %copy-start.2 = (bf16[8192,256]{1,0:T(8,128)(2,1)S(1)}, bf16[8192,256]{1,0:T(8,128)(2,1)}, u32[]{:S(2)}) copy-start(bf16[8192,256]{1,0:T(8,128)(2,1)} %param.8) | copy-start | bytes 12582916
  364.4 5.7 %copy-start.4 = (bf16[1024,8192]{1,0:T(8,128)(2,1)}, bf16[1024,8192]{1,0:T(8,128)(2,1)S(1)}, u32[]{:S(2)}) copy-start(bf16[1024,8192]{1,0:T(8,128)(2,1)S(1)} %multiply_convert_fusion) | copy-start | bytes 50331652
  375.7 176.9 %reduce-scatter.7.cloned.1.call-start = ((), (), s32[]{:S(2)}) async-start(), calls=%async_computation.4 | async-start | bytes 9437184
Sparse Core Ops, SparseCore 0:
  10.1 230.2 all-gather.1
  375.8 23.0 reduce-scatter.4
  403.6 149.0 reduce-scatter.6
